TPU v7x, 512 devices: a whole 4x4x16 slice. The times are simulated.
512 devices in a mesh: grid: 64 (over y, z), orb: 8 (over x, core).
Axes of the slice: x: 4, y: 4, z: 16, core: 2. Of those that a mesh axis runs over, the one named last changes fastest.
Arguments:
- orbitals: float32 [128, 32, 32, 1024], P('grid', None, None, 'orb'), may hold values from -14 to 14
- potential: float32 [128, 1024], P('grid'), may hold values from -1.5 to 0.5
Outputs:
- filtered: float32 [128, 32, 32, 1024], P('grid', None, None, 'orb')
- factor: float32 [1024, 1024], P(None, 'orb')
All inputs are finite; a program needn't handle non-finite values.
Results may differ from a plain program's by a relative error of at most 0.00005.
Values sent between devices are 32-bit elements; how exact they have to be, the bound alone decides.
A program may use at most 64 MiB of HBM per device.

v0:
```python
import jax
import jax.numpy as jnp
from jax import lax
from jax.sharding import PartitionSpec as P

GX = 32
GY = 32


LOWER = 1.0
UPPER = 10.0
KINETIC = 0.5


def padded_2(value, sides, width):
    for axis, dim in sides:
        devices, length = (lax.axis_size(axis), value.shape[dim])
        up = [(i, (i + 1) % devices) for i in range(devices)]
        down = [(j, i) for i, j in up]
        last = lax.slice_in_dim(value, length - width, length, axis=dim)
        initial = lax.slice_in_dim(value, 0, width, axis=dim)
        before = lax.ppermute(last, axis, up)
        after = lax.ppermute(initial, axis, down)
        value = jnp.concatenate([before, value, after], axis=dim)
    return value


def plane_terms(wavefield, direction):
    near_sum = jnp.roll(wavefield, 1, direction) + jnp.roll(wavefield, -1, direction)
    far_sum = jnp.roll(wavefield, 2, direction) + jnp.roll(wavefield, -2, direction)
    return 2.5 * wavefield - 4.0 / 3.0 * near_sum + 1.0 / 12.0 * far_sum


def apply_operator(wavefield, potential_grid):
    padded = padded_2(wavefield, (("grid", 0),), 2)
    layers = wavefield.shape[0]
    near_sum = padded[3 : layers + 3] + padded[1 : layers + 1]
    far_sum = padded[4 : layers + 4] + padded[0:layers]
    depth_terms = 2.5 * wavefield - 4.0 / 3.0 * near_sum + 1.0 / 12.0 * far_sum
    kinetic = depth_terms + plane_terms(wavefield, 1) + plane_terms(wavefield, 2)
    return KINETIC * kinetic + potential_grid[:, :, :, None] * wavefield


def pair_product(left_block, right_block):
    return jnp.einsum(
        "zyxi,zyxj->ij",
        left_block,
        right_block,
        precision=lax.Precision.HIGHEST,
        preferred_element_type=jnp.float32,
    )


def local(orbitals, potential):
    potential_grid = potential.reshape(orbitals.shape[0], GY, GX)
    centre = 0.5 * (UPPER + LOWER)
    half_width = 0.5 * (UPPER - LOWER)
    previous = orbitals
    current = (apply_operator(orbitals, potential_grid) - centre * orbitals) / half_width
    following = (
        2.0 * (apply_operator(current, potential_grid) - centre * current) / half_width - previous
    )
    previous, current = (current, following)
    width = current.shape[3]
    block_count = lax.axis_size("orb")
    total_width = width * block_count
    own_index = lax.axis_index("orb")
    own_start = own_index * width
    slab_cells = current.shape[0] * current.shape[1] * current.shape[2]
    cell_count = slab_cells * lax.axis_size("grid")
    empty = jnp.zeros((total_width, total_width), jnp.float32)
    column = pair_product(lax.all_gather(current, "orb", axis=3, tiled=True), current)
    placed = lax.dynamic_update_slice_in_dim(empty, column, own_start, 1)
    correlation = lax.psum(placed, ("grid", "orb"))
    lower_factor = jnp.linalg.cholesky(correlation / cell_count)
    factor_block = lax.dynamic_slice_in_dim(lower_factor.T, own_start, width, 1)
    return (current, factor_block)


def solution(mesh):
    placed = (P("grid", None, None, "orb"), P("grid", None))
    return jax.shard_map(
        local,
        mesh=mesh,
        in_specs=placed,
        out_specs=(P("grid", None, None, "orb"), P(None, "orb")),
        check_vma=False,
    )
```

profile of v0, /device:TPU:1, one launch (start us, length us, event | category | flops | bytes accessed | tf_op | source)
XLA Modules:
  0.0 878.0 jit_solution(10718398628092975450)
XLA Ops:
  7.2 1.9 copy.48
  9.1 14.4 %collective-permute-start = (f32[2,32,32,128]{3,1,0,2:T(8,128)S(1)}, f32[2,32,32,128]{3,1,0,2:T(8,128)}, u32[]{:S(2)}, u32[]{:S(2)}) collective-permute-start(f32[2,32,32,128]{3,1,0,2:T(8,128)S(1)} %copy.48), channel_id=1, source_target_pairs={{8,0},{16,8},{24,16},{32,24},{40,32},{48,40},{56,48},{64,56},{72,6... | collective-permute-start | bytes 3145736 | tf_op jit(solution)/shard_map/ppermute | solution.py:23
  23.6 1.9 collective-permute-start.1
  25.5 1.2 fusion.82
  27.8 17.5 %collective-permute-done = f32[2,32,32,128]{3,1,0,2:T(8,128)} collective-permute-done((f32[2,32,32,128]{3,1,0,2:T(8,128)S(1)}, f32[2,32,32,128]{3,1,0,2:T(8,128)}, u32[]{:S(2)}, u32[]{:S(2)}) %collective-permute-start) | collective-permute-done | bytes 1048608 | tf_op jit(solution)/shard_map/ppermute | solution.py:23
  45.4 7.2 collective-permute-done.1
  52.6 3.6 broadcast_multiply_fusion.1
  56.6 1.9 collective-permute-start.2
  58.5 3.4 collective-permute-start.3
  62.7 18.6 %collective-permute-done.2 = f32[2,32,32,128]{3,1,0,2:T(8,128)S(1)} collective-permute-done((f32[2,32,32,128]{3,1,0,2:T(8,128)S(1)}, f32[2,32,32,128]{3,1,0,2:T(8,128)S(1)}, u32[]{:S(2)}, u32[]{:S(2)}) %collective-permute-start.2) | collective-permute-done | bytes 1048608 | tf_op jit(solution)/shard_map/ppermute | solution.py:23
  81.2 5.2 collective-permute-done.3
  86.5 3.8 fusion.13
  90.4 53.0 %all-gather.2.cloned.1.call-done = f32[2,32,32,1024]{3,1,0,2:T(8,128)} async-done(((f32[2,32,32,128]{3,1,0,2:T(8,128)}), f32[2,32,32,1024]{3,1,0,2:T(8,128)}) %all-gather.2.cloned.1.call-update) | async-done | bytes 8388624 | tf_op jit(solution)/shard_map/all_gather | solution.py:72
  143.4 2.5 broadcast_in_dim.5
  145.9 8.3 fusion.1
  154.2 1.6 copy.91
  155.8 487.3 %all-reduce.3.cloned.1.call-done = f32[1024,1024]{0,1:T(8,128)} async-done(((f32[1024,1024]{0,1:T(8,128)}), f32[1024,1024]{0,1:T(8,128)}) %all-reduce.3.cloned.1.call-update) | async-done | bytes 4194320 | tf_op jit(solution)/shard_map/psum | solution.py:74
  643.1 5.0 broadcast_multiply_fusion
  648.1 5.5 copy.75
  653.6 4.4 fusion
  658.1 1.9 copy-done.1
  660.0 11.7 %cholesky.222 = f32[128,128]{1,0:T(8,128)S(1)} custom-call(f32[128,128]{1,0:T(8,128)S(1)} %cholesky.577), custom_call_target="Cholesky" | custom-call | tf_op jit(solution)/shard_map/jit(cholesky)/cholesky | solution.py:75
  671.8 9.8 %custom-call.59 = f32[1,128,128]{1,2,0:T(8,128)S(1)} custom-call(f32[1,128,128]{2,1,0:T(8,128)S(1)} %get-tuple-element.53), custom_call_target="InvertDiagBlocksLowerTriangular" | custom-call | tf_op jit(solution)/shard_map/jit(cholesky)/cholesky | solution.py:75
  681.6 1.5 fusion.45
  683.1 1.6 convolution_subtract_fusion
  684.7 11.7 %cholesky.243 = f32[128,128]{1,0:T(8,128)S(1)} custom-call(f32[128,128]{1,0:T(8,128)S(1)} %cholesky.581), custom_call_target="Cholesky" | custom-call | tf_op jit(solution)/shard_map/jit(cholesky)/cholesky | solution.py:75
  697.3 2.5 cholesky.254
  699.8 9.8 %custom-call.60 = f32[1,128,128]{1,2,0:T(8,128)S(1)} custom-call(f32[1,128,128]{2,1,0:T(8,128)S(1)} %get-tuple-element.51), custom_call_target="InvertDiagBlocksLowerTriangular" | custom-call | tf_op jit(solution)/shard_map/jit(cholesky)/cholesky | solution.py:75
  709.6 0.8 constant_dynamic-update-slice_fusion.7
  710.4 0.6 constant_dynamic-update-slice_fusion.6
  711.0 1.3 convolution_dynamic-update-slice_fusion
  712.3 2.7 convolution_subtract_fusion.1
  715.1 11.7 %cholesky.466 = f32[128,128]{1,0:T(8,128)S(1)} custom-call(f32[128,128]{1,0:T(8,128)S(1)} %cholesky.586), custom_call_target="Cholesky" | custom-call | tf_op jit(solution)/shard_map/jit(cholesky)/cholesky | solution.py:75
  726.9 0.6 constant_dynamic-update-slice_fusion.4
  727.5 9.8 %custom-call.61 = f32[1,128,128]{1,2,0:T(8,128)S(1)} custom-call(f32[1,128,128]{2,1,0:T(8,128)S(1)} %get-tuple-element.49), custom_call_target="InvertDiagBlocksLowerTriangular" | custom-call | tf_op jit(solution)/shard_map/jit(cholesky)/cholesky | solution.py:75
  737.4 1.3 convolution_dynamic-update-slice_fusion.1
  738.6 3.3 convolution_subtract_fusion.2
  741.9 11.7 %cholesky.485 = f32[128,128]{1,0:T(8,128)S(1)} custom-call(f32[128,128]{1,0:T(8,128)S(1)} %cholesky.591), custom_call_target="Cholesky" | custom-call | tf_op jit(solution)/shard_map/jit(cholesky)/cholesky | solution.py:75
  753.8 0.6 constant_dynamic-update-slice_fusion.3
  754.4 9.8 %custom-call.62 = f32[1,128,128]{1,2,0:T(8,128)S(1)} custom-call(f32[1,128,128]{2,1,0:T(8,128)S(1)} %get-tuple-element.47), custom_call_target="InvertDiagBlocksLowerTriangular" | custom-call | tf_op jit(solution)/shard_map/jit(cholesky)/cholesky | solution.py:75
  764.2 1.1 convolution_dynamic-update-slice_fusion.2
  765.4 3.1 convolution_subtract_fusion.3
  768.5 11.9 %cholesky.504 = f32[128,128]{1,0:T(8,128)S(1)} custom-call(f32[128,128]{1,0:T(8,128)S(1)} %cholesky.596), custom_call_target="Cholesky" | custom-call | tf_op jit(solution)/shard_map/jit(cholesky)/cholesky | solution.py:75
  780.5 0.6 constant_dynamic-update-slice_fusion.2
  781.2 9.8 %custom-call.63 = f32[1,128,128]{1,2,0:T(8,128)S(1)} custom-call(f32[1,128,128]{2,1,0:T(8,128)S(1)} %get-tuple-element.45), custom_call_target="InvertDiagBlocksLowerTriangular" | custom-call | tf_op jit(solution)/shard_map/jit(cholesky)/cholesky | solution.py:75
  791.0 1.1 convolution_dynamic-update-slice_fusion.3
  792.1 3.1 convolution_subtract_fusion.4
  795.2 11.7 %cholesky.524 = f32[128,128]{1,0:T(8,128)S(1)} custom-call(f32[128,128]{1,0:T(8,128)S(1)} %cholesky.601), custom_call_target="Cholesky" | custom-call | tf_op jit(solution)/shard_map/jit(cholesky)/cholesky | solution.py:75
  807.7 9.8 %custom-call.64 = f32[1,128,128]{1,2,0:T(8,128)S(1)} custom-call(f32[1,128,128]{2,1,0:T(8,128)S(1)} %get-tuple-element.43), custom_call_target="InvertDiagBlocksLowerTriangular" | custom-call | tf_op jit(solution)/shard_map/jit(cholesky)/cholesky | solution.py:75
  817.5 1.0 convolution_dynamic-update-slice_fusion.4
  818.5 2.9 convolution_subtract_fusion.5
  821.4 11.7 %cholesky.544 = f32[128,128]{1,0:T(8,128)S(1)} custom-call(f32[128,128]{1,0:T(8,128)S(1)} %cholesky.606), custom_call_target="Cholesky" | custom-call | tf_op jit(solution)/shard_map/jit(cholesky)/cholesky | solution.py:75
  833.3 0.6 constant_dynamic-update-slice_fusion
  833.9 9.8 %custom-call.65 = f32[1,128,128]{1,2,0:T(8,128)S(1)} custom-call(f32[1,128,128]{2,1,0:T(8,128)S(1)} %get-tuple-element.41), custom_call_target="InvertDiagBlocksLowerTriangular" | custom-call | tf_op jit(solution)/shard_map/jit(cholesky)/cholesky | solution.py:75
  843.7 0.9 convolution_dynamic-update-slice_fusion.5
  844.6 2.1 convolution_subtract_fusion.6
  846.7 11.7 %cholesky.562 = f32[128,128]{1,0:T(8,128)S(1)} custom-call(f32[128,128]{1,0:T(8,128)S(1)} %convolution_subtract_fusion.6), custom_call_target="Cholesky" | custom-call | tf_op jit(solution)/shard_map/jit(cholesky)/cholesky | solution.py:75
  858.6 0.7 compare_reduce_fusion.5
  859.9 0.7 compare_reduce_fusion.3
  860.6 0.7 compare_reduce_fusion.2
  861.3 0.7 compare_reduce_fusion.1
  861.9 0.6 compare_reduce_fusion
  862.6 0.6 constant_dynamic-update-slice_fusion.5
  868.8 1.9 fusion.43
  (61 shorter events, 5.9 us)
Async XLA Ops:
  7.2 19.6 %copy-start.2 = (f32[2,32,32,128]{3,2,1,0:T(8,128)S(1)}, f32[2,32,32,128]{3,2,1,0:T(8,128)}, u32[]{:S(2)}) copy-start(f32[2,32,32,128]{3,2,1,0:T(8,128)} %param.2) | copy-start | bytes 3145732
  7.2 19.6 %copy-start.4 = (f32[2,1024]{1,0:T(2,128)S(1)}, f32[2,1024]{1,0:T(2,128)}, u32[]{:S(2)}) copy-start(f32[2,1024]{1,0:T(2,128)} %param.3) | copy-start | bytes 24580
  7.2 136.2 %all-gather.2.cloned.1.call-start = ((), (), s32[]{:S(2)}) async-start(), calls=%async_computation | async-start | bytes 9437184 | tf_op jit(solution)/shard_map/all_gather | solution.py:72
  9.1 36.2 %collective-permute-start = (f32[2,32,32,128]{3,1,0,2:T(8,128)S(1)}, f32[2,32,32,128]{3,1,0,2:T(8,128)}, u32[]{:S(2)}, u32[]{:S(2)}) collective-permute-start(f32[2,32,32,128]{3,1,0,2:T(8,128)S(1)} %copy.48), channel_id=1, source_target_pairs={{8,0},{16,8},{24,16},{32,24},{40,32},{48,40},{56,48},{64,56},{72,6... | collective-permute-start | bytes 3145736 | tf_op jit(solution)/shard_map/ppermute | solution.py:23
  23.6 29.0 %collective-permute-start.1 = (f32[2,32,32,128]{3,1,0,2:T(8,128)S(1)}, f32[2,32,32,128]{3,1,0,2:T(8,128)}, u32[]{:S(2)}, u32[]{:S(2)}) collective-permute-start(f32[2,32,32,128]{3,1,0,2:T(8,128)S(1)} %copy.48), channel_id=1, source_target_pairs={{0,8},{8,16},{16,24},{24,32},{32,40},{40,48},{48,56},{56,64},{64,7... | collective-permute-start | bytes 3145736 | tf_op jit(solution)/shard_map/ppermute | solution.py:22
  27.4 25.2 %copy-start.3 = (f32[2,32,30,128]{3,1,0,2:T(8,128)S(1)}, f32[2,32,30,128]{3,1,0,2:T(8,128)}, u32[]{:S(2)}) copy-start(f32[2,32,30,128]{3,1,0,2:T(8,128)} %get-tuple-element.39) | copy-start | bytes 2949124
  56.6 24.7 %collective-permute-start.2 = (f32[2,32,32,128]{3,1,0,2:T(8,128)S(1)}, f32[2,32,32,128]{3,1,0,2:T(8,128)S(1)}, u32[]{:S(2)}, u32[]{:S(2)}) collective-permute-start(f32[2,32,32,128]{3,1,0,2:T(8,128)S(1)} %get-tuple-element.6), channel_id=1, source_target_pairs={{8,0},{16,8},{24,16},{32,24},{40,32},{48,40},{56,48},{64,56},{72,6... | collective-permute-start | bytes 3145736 | tf_op jit(solution)/shard_map/ppermute | solution.py:23
  58.5 28.0 %collective-permute-start.3 = (f32[2,32,32,128]{3,1,0,2:T(8,128)S(1)}, f32[2,32,32,128]{3,1,0,2:T(8,128)S(1)}, u32[]{:S(2)}, u32[]{:S(2)}) collective-permute-start(f32[2,32,32,128]{3,1,0,2:T(8,128)S(1)} %get-tuple-element.6), channel_id=1, source_target_pairs={{0,8},{8,16},{16,24},{24,32},{32,40},{40,48},{48,56},{56,64},{64,7... | collective-permute-start | bytes 3145736 | tf_op jit(solution)/shard_map/ppermute | solution.py:22
  90.3 55.6 %copy-start = (f32[2,32,32,128]{3,1,0,2:T(8,128)S(1)}, f32[2,32,32,128]{3,1,0,2:T(8,128)}, u32[]{:S(2)}) copy-start(f32[2,32,32,128]{3,1,0,2:T(8,128)} %fusion.13) | copy-start | bytes 3145732
  90.3 552.8 %all-reduce.3.cloned.1.call-start = ((), (), s32[]{:S(2)}) async-start(), calls=%async_computation.1 | async-start | bytes 8388608 | tf_op jit(solution)/shard_map/psum | solution.py:74
  658.1 1.9 copy-start.1
Sparse Core Ops, SparseCore 0:
  90.5 52.9 all-gather.1
  154.3 488.7 all-reduce.2
where the time goes:
time: 887 us; the launch traced here: 878 us
  waiting for transfers between devices  589 us (66%)
  other arithmetic  186 us (21%)
  matrix products  35.3 us (4%)
  local copies, waits for them, and re-layouts  26 us (3%)
  starting transfers between devices  21.7 us (2%)
  between operations  19.9 us (2%)
    psum x1, waiting for transfers between devices, local(): correlation = lax.psum(placed, ('grid', 'orb'))  487 us
    another operation x30, other arithmetic, local(): lower_factor = jnp.linalg.cholesky(correlation / cell_count)  167 us
    all_gather x1, waiting for transfers between devices, local(): lax.all_gather(current, 'orb', axis=3, tiled=True)  53 us
    ppermute x2, waiting for transfers between devices, padded_2(): after = lax.ppermute(initial, axis, down)  36.1 us
    another operation x14, matrix products, local(): lower_factor = jnp.linalg.cholesky(correlation / cell_count)  27 us
  transfers between devices with their start and end apart: 6, of which 6 were waited for; matrix products, arithmetic and copies ran while one was open for 1% of the time, Pallas kernels for 0%

commit v1 on v0

--- a/solution.py
+++ b/solution.py
@@ -1,15 +1,273 @@
+import functools
+
 import jax
 import jax.numpy as jnp
 from jax import lax
+from jax.experimental import pallas as pl
+from jax.experimental.pallas import tpu as pltpu
 from jax.sharding import PartitionSpec as P
 
 GX = 32
 GY = 32
-
-
 LOWER = 1.0
 UPPER = 10.0
 KINETIC = 0.5
+
+SIZE_X = 4
+SIZE_Y = 4
+SIZE_Z = 16
+BLOCK = 128
+BLOCKS = 8
+KEPT = 5
+ROWS = KEPT * BLOCK
+PART_Y = ROWS // SIZE_Y
+PART_Z = 16
+OWNERS = PART_Y // PART_Z
+TOTAL = BLOCK * BLOCKS
+
+MESH = pl.DeviceIdType.MESH
+HIGHEST = lax.Precision.HIGHEST
+
+
+def factor_diagonal(work):
+    sub = lax.broadcasted_iota(jnp.int32, (8, 128), 0)
+    for p in range(16):
+        o = 8 * p
+        pl_ = work[o:o+8, 0:128]
+        pr_ = work[o:o+8, 128:256]
+        s = {}
+        for i in range(8):
+            for j in range(i, 8):
+                s[i, j] = jnp.broadcast_to(pl_[i:i+1, o+j:o+j+1], (8, 128))
+        r = [None]*8
+        u = {}
+        rows_l, rows_r = [], []
+        L, R = pl_, pr_
+        for k in range(8):
+            r[k] = lax.rsqrt(s[k, k])
+            for j in range(k+1, 8):
+                u[k, j] = s[k, j] * r[k]
+            for i in range(k+1, 8):
+                for j in range(i, 8):
+                    s[i, j] = s[i, j] - u[k, i] * u[k, j]
+            kl = jnp.broadcast_to(L[k:k+1, :], (8, 128)) * r[k]
+            kr = jnp.broadcast_to(R[k:k+1, :], (8, 128)) * r[k]
+            rows_l.append(kl); rows_r.append(kr)
+            if k < 7:
+                col = u[k, 7]
+                for i in range(6, k, -1):
+                    col = jnp.where(sub == i, u[k, i], col)
+                col = jnp.where(sub > k, col, 0.0)
+                L = L - col * kl
+                R = R - col * kr
+        outl, outr = rows_l[7], rows_r[7]
+        for k in range(6, -1, -1):
+            outl = jnp.where(sub == k, rows_l[k], outl)
+            outr = jnp.where(sub == k, rows_r[k], outr)
+        work[o:o+8, 0:128] = outl
+        work[o:o+8, 128:256] = outr
+        for v in range(p+1, 16):
+            a = 8 * v
+            wl = work[a:a+8, 0:128]
+            wr = work[a:a+8, 128:256]
+            c = [jnp.broadcast_to(wl[:, o+k:o+k+1], (8, 128)) for k in range(8)]
+            for k in range(8):
+                c[k] = c[k] * r[k]
+                for j in range(k+1, 8):
+                    c[j] = c[j] - u[k, j] * c[k]
+                wl = wl - c[k] * rows_l[k]
+                wr = wr - c[k] * rows_r[k]
+            work[a:a+8, 0:128] = wl
+            work[a:a+8, 128:256] = wr
+
+
+def block_place(row, column):
+    if column - row < KEPT:
+        return column, column - row
+    return row, row - column + BLOCKS
+
+
+def remote(src, dst, send, recv, device):
+    return pltpu.make_async_remote_copy(
+        src_ref=src, dst_ref=dst, send_sem=send, recv_sem=recv, device_id=device, device_id_type=MESH
+    )
+
+
+def factor_kernel(
+    scale, part_ref, out_ref, from_y, from_z, summed, result, whole, work,
+    send_y, recv_y, send_z, recv_z, send_gz, recv_gz, send_gy, recv_gy, send_x, recv_x, send_c, recv_c,
+):
+    g, b = lax.axis_index("grid"), lax.axis_index("orb")
+    y, z = g // SIZE_Z, g % SIZE_Z
+    x, core = b // 2, b % 2
+
+    def at_y(d):
+        return ((y + d) % SIZE_Y) * SIZE_Z + z, b
+
+    def at_z(d):
+        return y * SIZE_Z + (z + d) % SIZE_Z, b
+
+    def at_x(d):
+        return g, ((x + d) % SIZE_X) * 2 + core
+
+    sibling = (g, x * 2 + 1 - core)
+
+    barrier = pltpu.get_barrier_semaphore()
+    for d in range(1, SIZE_Y):
+        pl.semaphore_signal(barrier, inc=1, device_id=at_y(d), device_id_type=MESH)
+    for d in range(1, SIZE_Z):
+        pl.semaphore_signal(barrier, inc=1, device_id=at_z(d), device_id_type=MESH)
+    for d in range(1, SIZE_X):
+        pl.semaphore_signal(barrier, inc=1, device_id=at_x(d), device_id_type=MESH)
+    pl.semaphore_signal(barrier, inc=1, device_id=sibling, device_id_type=MESH)
+    pl.semaphore_wait(barrier, SIZE_Y + SIZE_Z + SIZE_X - 2)
+
+    copies = []
+    for d in range(1, SIZE_Y):
+        there = (y + d) % SIZE_Y
+        copies.append(remote(part_ref.at[pl.ds(there * PART_Y, PART_Y)], from_y.at[d - 1], send_y.at[d - 1], recv_y.at[d - 1], at_y(d)))
+        copies[-1].start()
+    for c in copies:
+        c.wait_recv()
+    summed[...] = part_ref[pl.ds(y * PART_Y, PART_Y), :] + from_y[0] + from_y[1] + from_y[2]
+
+    for d in range(1, SIZE_Z):
+        there = (z + d) % SIZE_Z
+
+        @pl.when(there < OWNERS)
+        def _():
+            remote(summed.at[pl.ds(there * PART_Z, PART_Z)], from_z.at[d - 1], send_z.at[d - 1], recv_z.at[d - 1], at_z(d)).start()
+
+    mine = result.at[b]
+
+    @pl.when(z < OWNERS)
+    def _():
+        for d in range(1, SIZE_Z):
+            remote(summed.at[pl.ds(0, PART_Z)], from_z.at[d - 1], send_z.at[d - 1], recv_z.at[d - 1], at_z(d)).wait_recv()
+        total = summed[pl.ds(z * PART_Z, PART_Z), :]
+        for d in range(1, SIZE_Z):
+            total = total + from_z[d - 1]
+        place = pl.ds(y * PART_Y + z * PART_Z, PART_Z)
+        result[b, place, :] = total * scale
+        for d in range(1, SIZE_Z):
+            remote(mine.at[place], mine.at[place], send_gz.at[d - 1], recv_gz.at[d - 1], at_z(d)).start()
+
+    for d in range(1, SIZE_Z):
+        source = (z + SIZE_Z - d) % SIZE_Z
+
+        @pl.when(source < OWNERS)
+        def _():
+            place = pl.ds(y * PART_Y + source * PART_Z, PART_Z)
+            remote(mine.at[place], mine.at[place], send_gz.at[d - 1], recv_gz.at[d - 1], at_z(d)).wait_recv()
+
+    for d in range(1, SIZE_Y):
+        place = pl.ds(y * PART_Y, PART_Y)
+        remote(mine.at[place], mine.at[place], send_gy.at[d - 1], recv_gy.at[d - 1], at_y(d)).start()
+    for d in range(1, SIZE_Y):
+        place = pl.ds(((y + SIZE_Y - d) % SIZE_Y) * PART_Y, PART_Y)
+        remote(mine.at[place], mine.at[place], send_gy.at[d - 1], recv_gy.at[d - 1], at_y(d)).wait_recv()
+
+    for d in range(1, SIZE_X):
+        remote(mine, mine, send_x.at[d - 1], recv_x.at[d - 1], at_x(d)).start()
+    remote(mine, mine, send_c.at[0], recv_c.at[0], sibling).start()
+    for d in range(1, SIZE_X):
+        other = ((x + SIZE_X - d) % SIZE_X) * 2 + core
+        remote(result.at[other], result.at[other], send_x.at[d - 1], recv_x.at[d - 1], at_x(d)).wait_recv()
+        remote(result.at[other], result.at[other], send_c.at[d], recv_c.at[d], sibling).start()
+    for d in range(SIZE_X):
+        other = ((x + SIZE_X - d) % SIZE_X) * 2 + 1 - core
+        remote(result.at[other], result.at[other], send_c.at[d], recv_c.at[d], sibling).wait_recv()
+
+    for i in range(BLOCKS):
+        for j in range(i, BLOCKS):
+            owner, place = block_place(i, j)
+            whole[i * BLOCK : (i + 1) * BLOCK, j * BLOCK : (j + 1) * BLOCK] = result[owner, place * BLOCK : (place + 1) * BLOCK, :]
+
+    cholesky(whole, work)
+    out_ref[...] = whole[:, pl.ds(pl.multiple_of(b * BLOCK, BLOCK), BLOCK)]
+
+    for d in range(1, SIZE_Y):
+        remote(from_y.at[0], from_y.at[0], send_y.at[d - 1], recv_y.at[d - 1], at_y(d)).wait_send()
+        remote(mine.at[pl.ds(0, PART_Y)], mine.at[pl.ds(0, PART_Y)], send_gy.at[d - 1], recv_gy.at[d - 1], at_y(d)).wait_send()
+    for d in range(1, SIZE_Z):
+        there = (z + d) % SIZE_Z
+
+        @pl.when(there < OWNERS)
+        def _():
+            remote(from_z.at[0], from_z.at[0], send_z.at[d - 1], recv_z.at[d - 1], at_z(d)).wait_send()
+
+        @pl.when(z < OWNERS)
+        def _():
+            remote(from_z.at[0], from_z.at[0], send_gz.at[d - 1], recv_gz.at[d - 1], at_z(d)).wait_send()
+
+    for d in range(1, SIZE_X):
+        remote(mine, mine, send_x.at[d - 1], recv_x.at[d - 1], at_x(d)).wait_send()
+    for d in range(SIZE_X):
+        remote(mine, mine, send_c.at[d], recv_c.at[d], sibling).wait_send()
+
+
+def cholesky(S, work):
+    row = lax.broadcasted_iota(jnp.int32, (BLOCK, BLOCK), 0)
+    column = lax.broadcasted_iota(jnp.int32, (BLOCK, BLOCK), 1)
+
+    def step(k, carry):
+        for kk in range(BLOCKS):
+
+            @pl.when(k == kk)
+            def _():
+                work[:, 0:BLOCK] = S[kk * BLOCK : (kk + 1) * BLOCK, kk * BLOCK : (kk + 1) * BLOCK]
+
+        work[:, BLOCK:] = jnp.where(row == column, 1.0, 0.0)
+        factor_diagonal(work)
+        for kk in range(BLOCKS):
+
+            @pl.when(k == kk)
+            def _():
+                lo, hi = kk * BLOCK, (kk + 1) * BLOCK
+                S[lo:hi, lo:hi] = jnp.where(column >= row, work[:, 0:BLOCK], 0.0)
+                if kk < BLOCKS - 1:
+                    inverse = jnp.where(column <= row, work[:, BLOCK:], 0.0)
+                    S[lo:hi, hi:] = jnp.dot(inverse, S[lo:hi, hi:], precision=HIGHEST, preferred_element_type=jnp.float32)
+                    for a in range(kk + 1, BLOCKS):
+                        left = S[lo:hi, a * BLOCK : (a + 1) * BLOCK]
+                        S[a * BLOCK : (a + 1) * BLOCK, a * BLOCK :] -= lax.dot_general(
+                            left, S[lo:hi, a * BLOCK :], (((0,), (0,)), ((), ())),
+                            precision=HIGHEST, preferred_element_type=jnp.float32,
+                        )
+
+        return carry
+
+    lax.fori_loop(0, BLOCKS, step, 0)
+    for a in range(1, BLOCKS):
+        S[a * BLOCK : (a + 1) * BLOCK, 0 : a * BLOCK] = jnp.zeros((BLOCK, a * BLOCK), jnp.float32)
+
+
+def summed_factor(part, cells):
+    dma = pltpu.SemaphoreType.DMA
+    return pl.pallas_call(
+        functools.partial(factor_kernel, 1.0 / cells),
+        out_shape=jax.ShapeDtypeStruct((TOTAL, BLOCK), jnp.float32),
+        in_specs=[pl.BlockSpec(memory_space=pltpu.VMEM)],
+        out_specs=pl.BlockSpec(memory_space=pltpu.VMEM),
+        scratch_shapes=[
+            pltpu.VMEM((SIZE_Y - 1, PART_Y, BLOCK), jnp.float32),
+            pltpu.VMEM((SIZE_Z - 1, PART_Z, BLOCK), jnp.float32),
+            pltpu.VMEM((PART_Y, BLOCK), jnp.float32),
+            pltpu.VMEM((BLOCKS, ROWS, BLOCK), jnp.float32),
+            pltpu.VMEM((TOTAL, TOTAL), jnp.float32),
+            pltpu.VMEM((BLOCK, 2 * BLOCK), jnp.float32),
+            dma((SIZE_Y - 1,)), dma((SIZE_Y - 1,)),
+            dma((SIZE_Z - 1,)), dma((SIZE_Z - 1,)),
+            dma((SIZE_Z - 1,)), dma((SIZE_Z - 1,)),
+            dma((SIZE_Y - 1,)), dma((SIZE_Y - 1,)),
+            dma((SIZE_X - 1,)), dma((SIZE_X - 1,)),
+            dma((SIZE_X,)), dma((SIZE_X,)),
+        ],
+        compiler_params=pltpu.CompilerParams(
+            collective_id=1, has_side_effects=True, vmem_limit_bytes=40 * 1024 * 1024
+        ),
+        name="summed_factor",
+    )(part)
 
 
 def padded_2(value, sides, width):
@@ -63,17 +321,15 @@
     previous, current = (current, following)
     width = current.shape[3]
     block_count = lax.axis_size("orb")
-    total_width = width * block_count
     own_index = lax.axis_index("orb")
-    own_start = own_index * width
-    slab_cells = current.shape[0] * current.shape[1] * current.shape[2]
-    cell_count = slab_cells * lax.axis_size("grid")
-    empty = jnp.zeros((total_width, total_width), jnp.float32)
+    cells = current.shape[0] * current.shape[1] * current.shape[2] * lax.axis_size("grid")
     column = pair_product(lax.all_gather(current, "orb", axis=3, tiled=True), current)
-    placed = lax.dynamic_update_slice_in_dim(empty, column, own_start, 1)
-    correlation = lax.psum(placed, ("grid", "orb"))
-    lower_factor = jnp.linalg.cholesky(correlation / cell_count)
-    factor_block = lax.dynamic_slice_in_dim(lower_factor.T, own_start, width, 1)
+    column = column.reshape(block_count, width, width)
+    parts = []
+    for j in range(KEPT):
+        block = lax.dynamic_index_in_dim(column, (own_index - j) % block_count, 0, keepdims=False)
+        parts.append(jnp.where(own_index >= j, block, block.T))
+    factor_block = summed_factor(jnp.concatenate(parts, axis=0), cells)
     return (current, factor_block)
 
 

time: 887 us -> 268 us (0.30)
  waiting for transfers between devices: 589 us -> 98.1 us
  other arithmetic: 186 us -> 7.44 us
  Pallas kernels: 0 us -> 100 us
  matrix products: 35.3 us -> 15.7 us
  local copies, waits for them, and re-layouts: 26 us -> 9.87 us
    psum x1 -> x0, waiting for transfers between devices: 487 us -> none  [local(): correlation = lax.psum(placed, ('grid', 'orb'))]
    another operation x30 -> x0, other arithmetic: 167 us -> none  [local(): lower_factor = jnp.linalg.cholesky(correlation / cell_count)]
    pallas_call x0 -> x1, Pallas kernels: none -> 100 us  [summed_factor(): pl.pallas_call(functools.partial(factor_kernel, 1.0 / cells), out_shape=j...]
    another operation x14 -> x0, matrix products: 27 us -> none  [local(): lower_factor = jnp.linalg.cholesky(correlation / cell_count)]
    div x2 -> x0, other arithmetic: 9.45 us -> none  [local(): lower_factor = jnp.linalg.cholesky(correlation / cell_count)]
    another operation x25 -> x0, local copies, waits for them, and re-layouts: 9.17 us -> none  [local(): lower_factor = jnp.linalg.cholesky(correlation / cell_count)]
  transfers between devices with their start and end apart: 6 -> 5, of which waited for: 6 -> 5; matrix products, arithmetic and copies ran while one was open for 1% -> 2% of each run, Pallas kernels for 0% -> 0%
where the time goes in v1:
time: 268 us
  Pallas kernels  100 us (37%)
  waiting for transfers between devices  98.1 us (37%)
  starting transfers between devices  21.8 us (8%)
  matrix products  15.7 us (6%)
  between operations  14.4 us (5%)
  local copies, waits for them, and re-layouts  9.87 us (4%)
  other arithmetic  7.44 us (3%)
    pallas_call x1, Pallas kernels, summed_factor(): pl.pallas_call(functools.partial(factor_kernel, 1.0 / cells), out_shape=j...  100 us
    all_gather x1, waiting for transfers between devices, local(): lax.all_gather(current, 'orb', axis=3, tiled=True)  50.2 us
    ppermute x2, waiting for transfers between devices, padded_2(): after = lax.ppermute(initial, axis, down)  35.4 us
    ppermute x2, starting transfers between devices, padded_2(): after = lax.ppermute(initial, axis, down)  16.3 us
    dot_general x1, matrix products, pair_product(): jnp.einsum('zyxi,zyxj->ij', left_block, right_block, precision=lax.Precis...  15.7 us
    ppermute x2, waiting for transfers between devices, padded_2(): before = lax.ppermute(last, axis, up)  12.5 us
    unnamed x10, local copies, waits for them, and re-layouts  5.91 us
    ppermute x2, starting transfers between devices, padded_2(): before = lax.ppermute(last, axis, up)  5.46 us
  transfers between devices with their start and end apart: 5, of which 5 were waited for; matrix products, arithmetic and copies ran while one was open for 2% of the time, Pallas kernels for 0%

profile of v1, /device:TPU:1, one launch (start us, length us, event | category | flops | bytes accessed | tf_op | source)
XLA Modules:
  0.0 267.8 jit_solution(624502303452626726)
XLA Ops:
  7.2 0.0 all-gather.2.cloned.1.call-start
  7.2 1.8 copy.41
  9.0 14.4 %collective-permute-start = (f32[2,32,32,128]{3,1,0,2:T(8,128)S(1)}, f32[2,32,32,128]{3,1,0,2:T(8,128)}, u32[]{:S(2)}, u32[]{:S(2)}) collective-permute-start(f32[2,32,32,128]{3,1,0,2:T(8,128)S(1)} %copy.41), channel_id=1, source_target_pairs={{8,0},{16,8},{24,16},{32,24},{40,32},{48,40},{56,48},{64,56},{72,6... | collective-permute-start | bytes 3145736 | tf_op jit(solution)/shard_map/ppermute | solution.py:281
  23.5 1.9 collective-permute-start.1
  25.4 0.3 fusion.56
  25.7 0.8 fusion.49
  26.5 0.8 mul.94
  27.3 0.1 copy.62
  27.5 0.1 copy.65
  27.6 0.2 fusion.54
  27.8 0.2 fusion.50
  28.0 0.2 fusion.52
  28.3 17.0 %collective-permute-done = f32[2,32,32,128]{3,1,0,2:T(8,128)} collective-permute-done((f32[2,32,32,128]{3,1,0,2:T(8,128)S(1)}, f32[2,32,32,128]{3,1,0,2:T(8,128)}, u32[]{:S(2)}, u32[]{:S(2)}) %collective-permute-start) | collective-permute-done | bytes 1048608 | tf_op jit(solution)/shard_map/ppermute | solution.py:281
  45.3 7.2 %collective-permute-done.1 = f32[2,32,32,128]{3,1,0,2:T(8,128)} collective-permute-done((f32[2,32,32,128]{3,1,0,2:T(8,128)S(1)}, f32[2,32,32,128]{3,1,0,2:T(8,128)}, u32[]{:S(2)}, u32[]{:S(2)}) %collective-permute-start.1) | collective-permute-done | bytes 1048608 | tf_op jit(solution)/shard_map/ppermute | solution.py:280
  52.5 3.5 %broadcast_multiply_fusion = (f32[2,32,32,128]{3,1,0,2:T(8,128)S(1)}, f32[2,32,32,128]{3,1,0,2:T(8,128)S(1)}) fusion(f32[2,32,32,128]{3,1,0,2:T(8,128)S(1)} %copy.41, f32[2,32,32]{1,0,2:T(2,128)S(1)} %copy.62, f32[2,32,2,128]{3,1,0,2:T(8,128)S(1)} %get-tuple-element.37, f32[2,32,30,128]{3,1,0,2:T(8,128)S(1)} %get-tuple-element.39, ...), kind=kLoop, calls=%fused_computation.48 | loop fusion | flops 9699328 | bytes 13639680 | tf_op jit(solution)/shard_map/div | solution.py:317
  56.0 0.0 copy-start
  56.1 0.3 fusion.41
  56.5 1.9 collective-permute-start.2
  58.4 3.5 %collective-permute-start.3 = (f32[2,32,32,128]{3,1,0,2:T(8,128)S(1)}, f32[2,32,32,128]{3,1,0,2:T(8,128)S(1)}, u32[]{:S(2)}, u32[]{:S(2)}) collective-permute-start(f32[2,32,32,128]{3,1,0,2:T(8,128)S(1)} %get-tuple-element.6), channel_id=1, source_target_pairs={{0,8},{8,16},{16,24},{24,32},{32,40},{40,48},{48,56},{56,64},{64,7... | collective-permute-start | bytes 3145736 | tf_op jit(solution)/shard_map/ppermute | solution.py:280
  61.9 0.3 fusion.43
  62.2 0.2 fusion.45
  62.5 0.2 fusion.47
  62.7 18.4 %collective-permute-done.2 = f32[2,32,32,128]{3,1,0,2:T(8,128)S(1)} collective-permute-done((f32[2,32,32,128]{3,1,0,2:T(8,128)S(1)}, f32[2,32,32,128]{3,1,0,2:T(8,128)S(1)}, u32[]{:S(2)}, u32[]{:S(2)}) %collective-permute-start.2) | collective-permute-done | bytes 1048608 | tf_op jit(solution)/shard_map/ppermute | solution.py:281
  81.1 5.2 %collective-permute-done.3 = f32[2,32,32,128]{3,1,0,2:T(8,128)S(1)} collective-permute-done((f32[2,32,32,128]{3,1,0,2:T(8,128)S(1)}, f32[2,32,32,128]{3,1,0,2:T(8,128)S(1)}, u32[]{:S(2)}, u32[]{:S(2)}) %collective-permute-start.3) | collective-permute-done | bytes 1048608 | tf_op jit(solution)/shard_map/ppermute | solution.py:280
  86.4 0.0 copy-done
  86.4 3.8 %fusion.10 = f32[2,32,32,128]{3,1,0,2:T(8,128)} fusion(f32[2,32,32,128]{3,1,0,2:T(8,128)S(1)} %get-tuple-element.6, f32[2,32,32,128]{3,1,0,2:T(8,128)S(1)} %collective-permute-done.3, f32[2,32,32,128]{3,1,0,2:T(8,128)S(1)} %collective-permute-done.2, f32[2,31,32,128]{3,1,0,2:T(8,128)S(1)} %get-tuple-element.21, f32[2,1,32,128]{3,1,0,2:T(1,128)S(1)} %get-tuple-element.23, ...), kind=kLoop, calls=%fused_computation.11 | loop fusion | flops 9961472 | bytes 14688256 | tf_op jit(solution)/shard_map/sub | solution.py:319
  90.2 0.0 all-gather.2.cloned.1.call-update
  90.3 2.8 %copy.77 = f32[2,32,32,128]{3,2,1,0:T(8,128)} copy(f32[2,32,32,128]{3,1,0,2:T(8,128)} %fusion.10) | data formatting | bytes 2097152
  93.2 50.2 %all-gather.2.cloned.1.call-done = f32[2,32,32,1024]{3,1,0,2:T(8,128)} async-done(((f32[2,32,32,128]{3,1,0,2:T(8,128)}), f32[2,32,32,1024]{3,1,0,2:T(8,128)}) %all-gather.2.cloned.1.call-update) | async-done | bytes 8388624 | tf_op jit(solution)/shard_map/all_gather | solution.py:326
  143.3 15.7 %fusion.57 = f32[1024,128,1,1]{1,0,3,2:T(8,128)S(1)} fusion(f32[2,32,32,1024]{3,1,0,2:T(8,128)} %all-gather.2.cloned.1.call-done, f32[2,32,32,128]{3,1,0,2:T(8,128)} %fusion.10), kind=kOutput, calls=%fused_computation.81 | convolution fusion | flops 3221225472 | bytes 9961472 | tf_op jit(solution)/shard_map/zyxi,zyxj->ij/dot_general | solution.py:303
  159.1 0.1 copy.79
  159.2 0.1 copy.80
  159.3 0.1 copy.81
  159.4 0.1 copy.82
  159.5 0.1 copy.83
  159.7 100.5 %summed_factor.1 = f32[1024,128]{1,0:T(8,128)S(1)} custom-call(f32[640,128]{1,0:T(8,128)S(1)} %fusion.35.part_ref), custom_call_target="tpu_custom_call" | custom-call | tf_op jit(solution)/shard_map/summed_factor/pallas_call | solution.py:247
  260.2 0.8 copy.95
  (16 shorter events, 0.3 us)
Async XLA Ops:
  7.2 136.2 %all-gather.2.cloned.1.call-start = ((), (), s32[]{:S(2)}) async-start(), calls=%async_computation | async-start | bytes 9437184 | tf_op jit(solution)/shard_map/all_gather | solution.py:326
  9.0 36.2 %collective-permute-start = (f32[2,32,32,128]{3,1,0,2:T(8,128)S(1)}, f32[2,32,32,128]{3,1,0,2:T(8,128)}, u32[]{:S(2)}, u32[]{:S(2)}) collective-permute-start(f32[2,32,32,128]{3,1,0,2:T(8,128)S(1)} %copy.41), channel_id=1, source_target_pairs={{8,0},{16,8},{24,16},{32,24},{40,32},{48,40},{56,48},{64,56},{72,6... | collective-permute-start | bytes 3145736 | tf_op jit(solution)/shard_map/ppermute | solution.py:281
  23.5 29.0 %collective-permute-start.1 = (f32[2,32,32,128]{3,1,0,2:T(8,128)S(1)}, f32[2,32,32,128]{3,1,0,2:T(8,128)}, u32[]{:S(2)}, u32[]{:S(2)}) collective-permute-start(f32[2,32,32,128]{3,1,0,2:T(8,128)S(1)} %copy.41), channel_id=1, source_target_pairs={{0,8},{8,16},{16,24},{24,32},{32,40},{40,48},{48,56},{56,64},{64,7... | collective-permute-start | bytes 3145736 | tf_op jit(solution)/shard_map/ppermute | solution.py:280
  56.0 30.3 %copy-start = (f32[2,32,32,128]{3,2,1,0:T(8,128)S(1)}, f32[2,32,32,128]{3,2,1,0:T(8,128)}, u32[]{:S(2)}) copy-start(f32[2,32,32,128]{3,2,1,0:T(8,128)} %param.2) | copy-start | bytes 3145732
  56.5 24.7 %collective-permute-start.2 = (f32[2,32,32,128]{3,1,0,2:T(8,128)S(1)}, f32[2,32,32,128]{3,1,0,2:T(8,128)S(1)}, u32[]{:S(2)}, u32[]{:S(2)}) collective-permute-start(f32[2,32,32,128]{3,1,0,2:T(8,128)S(1)} %get-tuple-element.6), channel_id=1, source_target_pairs={{8,0},{16,8},{24,16},{32,24},{40,32},{48,40},{56,48},{64,56},{72,6... | collective-permute-start | bytes 3145736 | tf_op jit(solution)/shard_map/ppermute | solution.py:281
  58.4 28.0 %collective-permute-start.3 = (f32[2,32,32,128]{3,1,0,2:T(8,128)S(1)}, f32[2,32,32,128]{3,1,0,2:T(8,128)S(1)}, u32[]{:S(2)}, u32[]{:S(2)}) collective-permute-start(f32[2,32,32,128]{3,1,0,2:T(8,128)S(1)} %get-tuple-element.6), channel_id=1, source_target_pairs={{0,8},{8,16},{16,24},{24,32},{32,40},{40,48},{48,56},{56,64},{64,7... | collective-permute-start | bytes 3145736 | tf_op jit(solution)/shard_map/ppermute | solution.py:280
Sparse Core Ops, SparseCore 0:
  90.4 52.9 all-gather.1

commit v2 on v1

--- a/solution.py
+++ b/solution.py
@@ -12,6 +12,8 @@
 LOWER = 1.0
 UPPER = 10.0
 KINETIC = 0.5
+CENTRE = 0.5 * (UPPER + LOWER)
+HALF_WIDTH = 0.5 * (UPPER - LOWER)
 
 SIZE_X = 4
 SIZE_Y = 4
@@ -24,6 +26,9 @@
 PART_Z = 16
 OWNERS = PART_Y // PART_Z
 TOTAL = BLOCK * BLOCKS
+
+CHUNKS = tuple((4 * i, 4) for i in range(7)) + ((28, 2), (30, 2))
+AHEAD = 3
 
 MESH = pl.DeviceIdType.MESH
 HIGHEST = lax.Precision.HIGHEST
@@ -83,8 +88,8 @@
 
 def block_place(row, column):
     if column - row < KEPT:
-        return column, column - row
-    return row, row - column + BLOCKS
+        return row, column - row
+    return column, row - column + BLOCKS
 
 
 def remote(src, dst, send, recv, device):
@@ -93,13 +98,39 @@
     )
 
 
+def add_slab(source, before, after, weight, y):
+    rows = [source[layer, y] for layer in range(2)]
+    scale = KINETIC / HALF_WIDTH
+    out = []
+    for layer in range(2):
+        own = rows[layer]
+        if layer == 0:
+            near = rows[1] + before[1, y]
+            far = before[0, y] + after[0, y]
+        else:
+            near = rows[0] + after[0, y]
+            far = before[1, y] + after[1, y]
+        near = near + (source[layer, (y + GY - 1) % GY] + source[layer, (y + 1) % GY])
+        far = far + (source[layer, (y + GY - 2) % GY] + source[layer, (y + 2) % GY])
+        near = near + (pltpu.roll(own, 1, 0) + pltpu.roll(own, GX - 1, 0))
+        far = far + (pltpu.roll(own, 2, 0) + pltpu.roll(own, GX - 2, 0))
+        out.append(weight[layer, y] * own - (4.0 / 3.0 * scale) * near + (1.0 / 12.0 * scale) * far)
+    return out
+
+
 def factor_kernel(
-    scale, part_ref, out_ref, from_y, from_z, summed, result, whole, work,
+    scale, orbitals_ref, potential_ref, filtered_ref, out_ref,
+    weight, slab, before, after, current, before_2, after_2, filtered, gathered, relay, part,
+    from_y, from_z, summed, result, whole, work,
+    local_sem, send_h, recv_h, send_k, recv_k, send_o, recv_o, send_s, recv_s,
     send_y, recv_y, send_z, recv_z, send_gz, recv_gz, send_gy, recv_gy, send_x, recv_x, send_c, recv_c,
 ):
     g, b = lax.axis_index("grid"), lax.axis_index("orb")
     y, z = g // SIZE_Z, g % SIZE_Z
     x, core = b // 2, b % 2
+    slabs = SIZE_Y * SIZE_Z
+    ahead, behind = ((g + 1) % slabs, b), ((g + slabs - 1) % slabs, b)
+    count = len(CHUNKS)
 
     def at_y(d):
         return ((y + d) % SIZE_Y) * SIZE_Z + z, b
@@ -113,23 +144,168 @@
     sibling = (g, x * 2 + 1 - core)
 
     barrier = pltpu.get_barrier_semaphore()
+    for device in (ahead, behind):
+        pl.semaphore_signal(barrier, inc=1, device_id=device, device_id_type=MESH)
+    for d in range(1, SIZE_X):
+        pl.semaphore_signal(barrier, inc=1, device_id=at_x(d), device_id_type=MESH)
+    pl.semaphore_signal(barrier, inc=1, device_id=sibling, device_id_type=MESH)
     for d in range(1, SIZE_Y):
         pl.semaphore_signal(barrier, inc=1, device_id=at_y(d), device_id_type=MESH)
     for d in range(1, SIZE_Z):
         pl.semaphore_signal(barrier, inc=1, device_id=at_z(d), device_id_type=MESH)
-    for d in range(1, SIZE_X):
-        pl.semaphore_signal(barrier, inc=1, device_id=at_x(d), device_id_type=MESH)
-    pl.semaphore_signal(barrier, inc=1, device_id=sibling, device_id_type=MESH)
-    pl.semaphore_wait(barrier, SIZE_Y + SIZE_Z + SIZE_X - 2)
+    load = pltpu.make_async_copy(orbitals_ref, slab, local_sem.at[0])
+    load.start()
+    pl.semaphore_wait(barrier, SIZE_Y + SIZE_Z + SIZE_X)
+
+    def rows(k):
+        return pl.ds(CHUNKS[k][0], CHUNKS[k][1])
+
+    def halo(source, low, high, send, recv, k):
+        return (
+            remote(source.at[:, rows(k)], low.at[:, rows(k)], send.at[0, k], recv.at[0, k], ahead),
+            remote(source.at[:, rows(k)], high.at[:, rows(k)], send.at[1, k], recv.at[1, k], behind),
+        )
+
+    def first_halo(k):
+        return halo(orbitals_ref, before, after, send_h, recv_h, k)
+
+    def second_halo(k):
+        return halo(current, before_2, after_2, send_k, recv_k, k)
+
+    def to_left(k):
+        return remote(filtered.at[:, rows(k)], gathered.at[1, :, rows(k)], send_o.at[0, k], recv_o.at[0, k], at_x(SIZE_X - 1))
+
+    def to_right(k):
+        return remote(filtered.at[1, rows(k)], relay.at[rows(k)], send_o.at[1, k], recv_o.at[1, k], at_x(1))
+
+    def on_left(k):
+        return remote(gathered.at[1, 0, rows(k)], gathered.at[3, 0, rows(k)], send_o.at[2, k], recv_o.at[2, k], at_x(SIZE_X - 1))
+
+    def on_right(k):
+        return remote(relay.at[rows(k)], gathered.at[3, 1, rows(k)], send_o.at[3, k], recv_o.at[3, k], at_x(1))
+
+    def across(source, slot, k):
+        return remote(source.at[:, rows(k)], gathered.at[2 * slot, :, rows(k)], send_s.at[slot, k], recv_s.at[slot, k], sibling)
+
+    def store(k):
+        return pltpu.make_async_copy(filtered.at[:, rows(k)], filtered_ref.at[:, rows(k)], local_sem.at[1 + k])
+
+    for k in range(AHEAD):
+        for copy in first_halo(k):
+            copy.start()
+
+    table = potential_ref[...]
+    for i in range(2 * GY):
+        weight[i // GY, i % GY] = (jnp.broadcast_to(table[:, i : i + 1], (GX, BLOCK)) + (7.5 * KINETIC - CENTRE)) * (1.0 / HALF_WIDTH)
+    part[...] = jnp.zeros_like(part)
+    load.wait()
+
+    def first_step(k):
+        for copy in first_halo(k):
+            copy.wait_recv()
+        start, height = CHUNKS[k]
+
+        def line(i, carry):
+            for layer, value in enumerate(add_slab(slab, before, after, weight, start + i)):
+                current[layer, start + i] = value
+            return carry
+
+        lax.fori_loop(0, height, line, 0)
+        for copy in second_halo(k):
+            copy.start()
+        if k + AHEAD < count:
+            for copy in first_halo(k + AHEAD):
+                copy.start()
+
+    def second_step(k):
+        for copy in second_halo(k):
+            copy.wait_recv()
+        start, height = CHUNKS[k]
+
+        def line(i, carry):
+            for layer, value in enumerate(add_slab(current, before_2, after_2, weight, start + i)):
+                filtered[layer, start + i] = 2.0 * value - slab[layer, start + i]
+            return carry
+
+        lax.fori_loop(0, height, line, 0)
+        to_left(k).start()
+        to_right(k).start()
+
+        @pl.when(core == 1)
+        def _():
+            across(filtered, 0, k).start()
+
+        store(k).start()
+
+    def pass_on(k):
+        to_left(k).wait_recv()
+        on_left(k).start()
+        to_right(k).wait_recv()
+        on_right(k).start()
+
+        @pl.when(core == 1)
+        def _():
+            across(gathered.at[1], 1, k).start()
+
+        @pl.when(core == 0)
+        def _():
+            across(gathered.at[1], 0, k).start()
+
+    def share(k):
+        on_left(k).wait_recv()
+        on_right(k).wait_recv()
+
+        @pl.when(core == 0)
+        def _():
+            across(gathered.at[3], 1, k).start()
+
+    def multiply(k):
+        across(filtered, 0, k).wait_recv()
+        across(filtered, 1, k).wait_recv()
+        cells = 2 * CHUNKS[k][1] * GX
+        own = filtered[:, rows(k)].reshape(cells, BLOCK)
+        others = [own] + [gathered[j, :, rows(k)].reshape(cells, BLOCK) for j in range(KEPT - 1)]
+        product = lax.dot_general(
+            own, jnp.concatenate(others, axis=1), (((0,), (0,)), ((), ())),
+            precision=HIGHEST, preferred_element_type=jnp.float32,
+        )
+        for j in range(KEPT):
+            part[j * BLOCK : (j + 1) * BLOCK, :] += product[:, j * BLOCK : (j + 1) * BLOCK]
+
+    stages = (second_step, pass_on, share, multiply)
+    order = []
+
+    def advance(k):
+        order.append(k)
+        for lag, stage in enumerate(stages):
+            place = len(order) - 1 - lag
+            if 0 <= place < count and order[place] is not None:
+                stage(order[place])
+
+    for k in range(count):
+        first_step(k)
+        if k - AHEAD >= 1:
+            advance(k - AHEAD)
+    advance(0)
+    for k in range(count - AHEAD, count):
+        advance(k)
+    for lag in range(1, len(stages)):
+        advance(None)
+
+    for j in range(1, KEPT):
+
+        @pl.when(b + j >= BLOCKS)
+        def _():
+            part[j * BLOCK : (j + 1) * BLOCK, :] = part[j * BLOCK : (j + 1) * BLOCK, :].T
 
     copies = []
     for d in range(1, SIZE_Y):
         there = (y + d) % SIZE_Y
-        copies.append(remote(part_ref.at[pl.ds(there * PART_Y, PART_Y)], from_y.at[d - 1], send_y.at[d - 1], recv_y.at[d - 1], at_y(d)))
+        copies.append(remote(part.at[pl.ds(there * PART_Y, PART_Y)], from_y.at[d - 1], send_y.at[d - 1], recv_y.at[d - 1], at_y(d)))
         copies[-1].start()
     for c in copies:
         c.wait_recv()
-    summed[...] = part_ref[pl.ds(y * PART_Y, PART_Y), :] + from_y[0] + from_y[1] + from_y[2]
+    summed[...] = part[pl.ds(y * PART_Y, PART_Y), :] + from_y[0] + from_y[1] + from_y[2]
 
     for d in range(1, SIZE_Z):
         there = (z + d) % SIZE_Z
@@ -200,6 +376,12 @@
         def _():
             remote(from_z.at[0], from_z.at[0], send_gz.at[d - 1], recv_gz.at[d - 1], at_z(d)).wait_send()
 
+    for k in range(count):
+        for copy in (*first_halo(k), *second_halo(k), to_left(k), to_right(k), on_left(k), on_right(k)):
+            copy.wait_send()
+        for slot in range(2):
+            across(filtered, slot, k).wait_send()
+        store(k).wait()
     for d in range(1, SIZE_X):
         remote(mine, mine, send_x.at[d - 1], recv_x.at[d - 1], at_x(d)).wait_send()
     for d in range(SIZE_X):
@@ -242,20 +424,34 @@
         S[a * BLOCK : (a + 1) * BLOCK, 0 : a * BLOCK] = jnp.zeros((BLOCK, a * BLOCK), jnp.float32)
 
 
-def summed_factor(part, cells):
+def filtered_factor(orbitals, potential, cells):
     dma = pltpu.SemaphoreType.DMA
+    field = pltpu.VMEM((2, GY, GX, BLOCK), jnp.float32)
+    count = len(CHUNKS)
     return pl.pallas_call(
         functools.partial(factor_kernel, 1.0 / cells),
-        out_shape=jax.ShapeDtypeStruct((TOTAL, BLOCK), jnp.float32),
-        in_specs=[pl.BlockSpec(memory_space=pltpu.VMEM)],
-        out_specs=pl.BlockSpec(memory_space=pltpu.VMEM),
+        out_shape=(
+            jax.ShapeDtypeStruct((2, GY, GX, BLOCK), jnp.float32),
+            jax.ShapeDtypeStruct((TOTAL, BLOCK), jnp.float32),
+        ),
+        in_specs=[pl.BlockSpec(memory_space=pl.ANY), pl.BlockSpec(memory_space=pltpu.VMEM)],
+        out_specs=(pl.BlockSpec(memory_space=pl.ANY), pl.BlockSpec(memory_space=pltpu.VMEM)),
         scratch_shapes=[
+            field, field, field, field, field, field, field, field,
+            pltpu.VMEM((KEPT - 1, 2, GY, GX, BLOCK), jnp.float32),
+            pltpu.VMEM((GY, GX, BLOCK), jnp.float32),
+            pltpu.VMEM((ROWS, BLOCK), jnp.float32),
             pltpu.VMEM((SIZE_Y - 1, PART_Y, BLOCK), jnp.float32),
             pltpu.VMEM((SIZE_Z - 1, PART_Z, BLOCK), jnp.float32),
             pltpu.VMEM((PART_Y, BLOCK), jnp.float32),
             pltpu.VMEM((BLOCKS, ROWS, BLOCK), jnp.float32),
             pltpu.VMEM((TOTAL, TOTAL), jnp.float32),
             pltpu.VMEM((BLOCK, 2 * BLOCK), jnp.float32),
+            dma((1 + count,)),
+            dma((2, count)), dma((2, count)),
+            dma((2, count)), dma((2, count)),
+            dma((4, count)), dma((4, count)),
+            dma((2, count)), dma((2, count)),
             dma((SIZE_Y - 1,)), dma((SIZE_Y - 1,)),
             dma((SIZE_Z - 1,)), dma((SIZE_Z - 1,)),
             dma((SIZE_Z - 1,)), dma((SIZE_Z - 1,)),
@@ -264,73 +460,15 @@
             dma((SIZE_X,)), dma((SIZE_X,)),
         ],
         compiler_params=pltpu.CompilerParams(
-            collective_id=1, has_side_effects=True, vmem_limit_bytes=40 * 1024 * 1024
+            collective_id=1, has_side_effects=True, vmem_limit_bytes=48 * 1024 * 1024
         ),
-        name="summed_factor",
-    )(part)
-
-
-def padded_2(value, sides, width):
-    for axis, dim in sides:
-        devices, length = (lax.axis_size(axis), value.shape[dim])
-        up = [(i, (i + 1) % devices) for i in range(devices)]
-        down = [(j, i) for i, j in up]
-        last = lax.slice_in_dim(value, length - width, length, axis=dim)
-        initial = lax.slice_in_dim(value, 0, width, axis=dim)
-        before = lax.ppermute(last, axis, up)
-        after = lax.ppermute(initial, axis, down)
-        value = jnp.concatenate([before, value, after], axis=dim)
-    return value
-
-
-def plane_terms(wavefield, direction):
-    near_sum = jnp.roll(wavefield, 1, direction) + jnp.roll(wavefield, -1, direction)
-    far_sum = jnp.roll(wavefield, 2, direction) + jnp.roll(wavefield, -2, direction)
-    return 2.5 * wavefield - 4.0 / 3.0 * near_sum + 1.0 / 12.0 * far_sum
-
-
-def apply_operator(wavefield, potential_grid):
-    padded = padded_2(wavefield, (("grid", 0),), 2)
-    layers = wavefield.shape[0]
-    near_sum = padded[3 : layers + 3] + padded[1 : layers + 1]
-    far_sum = padded[4 : layers + 4] + padded[0:layers]
-    depth_terms = 2.5 * wavefield - 4.0 / 3.0 * near_sum + 1.0 / 12.0 * far_sum
-    kinetic = depth_terms + plane_terms(wavefield, 1) + plane_terms(wavefield, 2)
-    return KINETIC * kinetic + potential_grid[:, :, :, None] * wavefield
-
-
-def pair_product(left_block, right_block):
-    return jnp.einsum(
-        "zyxi,zyxj->ij",
-        left_block,
-        right_block,
-        precision=lax.Precision.HIGHEST,
-        preferred_element_type=jnp.float32,
-    )
+        name="filtered_factor",
+    )(orbitals, potential)
 
 
 def local(orbitals, potential):
-    potential_grid = potential.reshape(orbitals.shape[0], GY, GX)
-    centre = 0.5 * (UPPER + LOWER)
-    half_width = 0.5 * (UPPER - LOWER)
-    previous = orbitals
-    current = (apply_operator(orbitals, potential_grid) - centre * orbitals) / half_width
-    following = (
-        2.0 * (apply_operator(current, potential_grid) - centre * current) / half_width - previous
-    )
-    previous, current = (current, following)
-    width = current.shape[3]
-    block_count = lax.axis_size("orb")
-    own_index = lax.axis_index("orb")
-    cells = current.shape[0] * current.shape[1] * current.shape[2] * lax.axis_size("grid")
-    column = pair_product(lax.all_gather(current, "orb", axis=3, tiled=True), current)
-    column = column.reshape(block_count, width, width)
-    parts = []
-    for j in range(KEPT):
-        block = lax.dynamic_index_in_dim(column, (own_index - j) % block_count, 0, keepdims=False)
-        parts.append(jnp.where(own_index >= j, block, block.T))
-    factor_block = summed_factor(jnp.concatenate(parts, axis=0), cells)
-    return (current, factor_block)
+    cells = orbitals.shape[0] * GY * GX * SIZE_Y * SIZE_Z
+    return filtered_factor(orbitals, potential.reshape(-1, GX).T, cells)
 
 
 def solution(mesh):

time: 268 us -> 185 us (0.69)
  waiting for transfers between devices: 98.1 us -> 0 us
  Pallas kernels: 100 us -> 180 us
  starting transfers between devices: 21.8 us -> 0 us
  matrix products: 15.7 us -> 0 us
  between operations: 14.4 us -> 0.64 us
  other arithmetic: 7.44 us -> 0 us
  local copies, waits for them, and re-layouts: 9.87 us -> 3.85 us
    pallas_call x1, Pallas kernels: 100 us -> 180 us  [filtered_factor(): pl.pallas_call(functools.partial(factor_kernel, 1.0 / cells), out_shape=(...]
    all_gather x1 -> x0, waiting for transfers between devices: 50.2 us -> none  [local(): lax.all_gather(current, 'orb', axis=3, tiled=True)]
    ppermute x4 -> x0, waiting for transfers between devices: 47.9 us -> none  [the longest x2 35.4 us: padded_2(): after = lax.ppermute(initial, axis, down)]
    ppermute x4 -> x0, starting transfers between devices: 21.8 us -> none  [the longest x2 16.3 us: padded_2(): after = lax.ppermute(initial, axis, down)]
    dot_general x1 -> x0, matrix products: 15.7 us -> none  [pair_product(): jnp.einsum('zyxi,zyxj->ij', left_block, right_block, precision=lax.Precis...]
    sub x1 -> x0, other arithmetic: 3.84 us -> none  [local(): 2.0 * (apply_operator(current, potential_grid) - centre * current)]
    div x1 -> x0, other arithmetic: 3.55 us -> none  [local(): (apply_operator(orbitals, potential_grid) - centre * orbitals) / half_width]
    slice x18 -> x0, local copies, waits for them, and re-layouts: 2.99 us -> none  [the longest x5 1.28 us: plane_terms(): jnp.roll(wavefield, 1, direction) + jnp.roll(wavefield, -1, direction)]
  transfers between devices with their start and end apart: 5 -> 0, of which waited for: 5 -> 0; matrix products, arithmetic and copies ran while one was open for 2% -> 0% of each run, Pallas kernels for 0% -> 0%
where the time goes in v2:
time: 185 us; the launch traced here: 184 us
  Pallas kernels  180 us (97%)
  local copies, waits for them, and re-layouts  3.85 us (2%)
    pallas_call x1, Pallas kernels, filtered_factor(): pl.pallas_call(functools.partial(factor_kernel, 1.0 / cells), out_shape=(...  180 us

profile of v2, /device:TPU:1, one launch (start us, length us, event | category | flops | bytes accessed | tf_op | source)
XLA Modules:
  0.0 184.3 jit_solution(1573380798544282319)
XLA Ops:
  0.6 0.8 reshape.7
  1.4 0.1 copy.4
  1.5 0.0 copy-start
  1.5 1.2 copy-done
  2.7 179.8 %filtered_factor.1 = (f32[2,32,32,128]{3,2,1,0:T(8,128)S(1)}, f32[1024,128]{1,0:T(8,128)S(1)}) custom-call(f32[2,32,32,128]{3,2,1,0:T(8,128)S(1)} %copy-done, f32[32,64]{1,0:T(8,128)S(1)} %bitcast.1), custom_call_target="tpu_custom_call" | custom-call | tf_op jit(solution)/shard_map/filtered_factor/pallas_call | solution.py:431
  182.6 1.0 copy.7
  183.5 0.8 copy.8
Async XLA Ops:
  1.5 1.2 copy-start

commit v3 on v2

--- a/solution.py
+++ b/solution.py
@@ -25,10 +25,11 @@
 PART_Y = ROWS // SIZE_Y
 PART_Z = 16
 OWNERS = PART_Y // PART_Z
+GROUP = 4
 TOTAL = BLOCK * BLOCKS
 
 CHUNKS = tuple((4 * i, 4) for i in range(7)) + ((28, 2), (30, 2))
-AHEAD = 3
+AHEAD = 2
 
 MESH = pl.DeviceIdType.MESH
 HIGHEST = lax.Precision.HIGHEST
@@ -41,9 +42,10 @@
         pl_ = work[o:o+8, 0:128]
         pr_ = work[o:o+8, 128:256]
         s = {}
-        for i in range(8):
-            for j in range(i, 8):
-                s[i, j] = jnp.broadcast_to(pl_[i:i+1, o+j:o+j+1], (8, 128))
+        for j in range(8):
+            column = jnp.broadcast_to(pl_[:, o+j:o+j+1], (8, 128))
+            for i in range(j + 1):
+                s[i, j] = jnp.broadcast_to(column[i:i+1, :], (8, 128))
         r = [None]*8
         u = {}
         rows_l, rows_r = [], []
@@ -194,9 +196,12 @@
         for copy in first_halo(k):
             copy.start()
 
-    table = potential_ref[...]
-    for i in range(2 * GY):
-        weight[i // GY, i % GY] = (jnp.broadcast_to(table[:, i : i + 1], (GX, BLOCK)) + (7.5 * KINETIC - CENTRE)) * (1.0 / HALF_WIDTH)
+    lines = BLOCK // GX
+    for layer in range(2):
+        for i in range(GY // lines):
+            cells = potential_ref[layer : layer + 1, i * BLOCK : (i + 1) * BLOCK] + (7.5 * KINETIC - CENTRE)
+            turned = jnp.broadcast_to(cells * (1.0 / HALF_WIDTH), (BLOCK, BLOCK)).T
+            weight[layer, i * lines : (i + 1) * lines] = turned.reshape(lines, GX, BLOCK)
     part[...] = jnp.zeros_like(part)
     load.wait()
 
@@ -307,14 +312,23 @@
         c.wait_recv()
     summed[...] = part[pl.ds(y * PART_Y, PART_Y), :] + from_y[0] + from_y[1] + from_y[2]
 
-    for d in range(1, SIZE_Z):
+    for d in sorted(range(1, SIZE_Z), key=lambda d: -min(d, SIZE_Z - d)):
         there = (z + d) % SIZE_Z
 
         @pl.when(there < OWNERS)
         def _():
             remote(summed.at[pl.ds(there * PART_Z, PART_Z)], from_z.at[d - 1], send_z.at[d - 1], recv_z.at[d - 1], at_z(d)).start()
 
-    mine = result.at[b]
+    def piece(source):
+        return result.at[x, core, y, source // GROUP, source // 2 % 2, source % 2]
+
+    def far(source, d):
+        return remote(piece(source), piece(source), send_gz.at[0, d - 1], recv_gz.at[0, d - 1], at_z(GROUP * d))
+
+    def near(member, d, full):
+        place = (z + d) % GROUP - z % GROUP
+        pieces = result.at[x, core, y, :, 0, member % 2] if full else result.at[x, core, y, 0:2, 1, member % 2]
+        return remote(pieces, pieces, send_gz.at[1, d - 1], recv_gz.at[1, d - 1], (g + place, b))
 
     @pl.when(z < OWNERS)
     def _():
@@ -323,48 +337,106 @@
         total = summed[pl.ds(z * PART_Z, PART_Z), :]
         for d in range(1, SIZE_Z):
             total = total + from_z[d - 1]
-        place = pl.ds(y * PART_Y + z * PART_Z, PART_Z)
-        result[b, place, :] = total * scale
-        for d in range(1, SIZE_Z):
-            remote(mine.at[place], mine.at[place], send_gz.at[d - 1], recv_gz.at[d - 1], at_z(d)).start()
-
-    for d in range(1, SIZE_Z):
-        source = (z + SIZE_Z - d) % SIZE_Z
+        result[x, core, y, z // GROUP, z // 2 % 2, z % 2] = total * scale
+        for d in (2, 1, 3):
+            far(z, d).start()
+
+    for d in range(1, SIZE_Z // GROUP):
+        source = (z + SIZE_Z - GROUP * d) % SIZE_Z
 
         @pl.when(source < OWNERS)
         def _():
-            place = pl.ds(y * PART_Y + source * PART_Z, PART_Z)
-            remote(mine.at[place], mine.at[place], send_gz.at[d - 1], recv_gz.at[d - 1], at_z(d)).wait_recv()
-
+            far(source, d).wait_recv()
+
+    for full in (True, False):
+
+        @pl.when((z % GROUP < 2) == full)
+        def _():
+            for d in (2, 1, 3):
+                near(z % GROUP, d, full).start()
+
+    for d in range(1, GROUP):
+        member = (z + GROUP - d) % GROUP
+        for full in (True, False):
+
+            @pl.when((member < 2) == full)
+            def _():
+                near(member, d, full).wait_recv()
+
+    def first_x(d, source):
+        ref = result.at[source, core, y, :, 0]
+        return remote(ref, ref, send_x.at[0, d - 1], recv_x.at[0, d - 1], at_x(d))
+
+    def first_y(d, source):
+        ref = result.at[x, core, source, 0:2, 1]
+        return remote(ref, ref, send_gy.at[0, d - 1], recv_gy.at[0, d - 1], at_y(d))
+
+    def then_y(d, source):
+        ref = result.at[:, core, source, :, 0]
+        return remote(ref, ref, send_gy.at[1, d - 1], recv_gy.at[1, d - 1], at_y(d))
+
+    def then_x(d, source):
+        ref = result.at[source, core, :, 0:2, 1]
+        return remote(ref, ref, send_x.at[1, d - 1], recv_x.at[1, d - 1], at_x(d))
+
+    def share_y(d, owner):
+        ref = result.at[:, owner, (y + SIZE_Y - d) % SIZE_Y, :, 0]
+        return remote(ref, ref, send_c.at[0, d], recv_c.at[0, d], sibling)
+
+    def share_x(d, owner):
+        ref = result.at[(x + SIZE_X - d) % SIZE_X, owner, :, 0:2, 1]
+        return remote(ref, ref, send_c.at[1, d], recv_c.at[1, d], sibling)
+
+    def before_x(d):
+        return (x + SIZE_X - d) % SIZE_X
+
+    def before_y(d):
+        return (y + SIZE_Y - d) % SIZE_Y
+
+    for d in (2, 1, 3):
+        first_x(d, x).start()
+        first_y(d, y).start()
+    for d in range(1, SIZE_X):
+        first_x(d, before_x(d)).wait_recv()
+    for d in (2, 1, 3):
+        then_y(d, y).start()
+    share_y(0, core).start()
     for d in range(1, SIZE_Y):
-        place = pl.ds(y * PART_Y, PART_Y)
-        remote(mine.at[place], mine.at[place], send_gy.at[d - 1], recv_gy.at[d - 1], at_y(d)).start()
-    for d in range(1, SIZE_Y):
-        place = pl.ds(((y + SIZE_Y - d) % SIZE_Y) * PART_Y, PART_Y)
-        remote(mine.at[place], mine.at[place], send_gy.at[d - 1], recv_gy.at[d - 1], at_y(d)).wait_recv()
-
-    for d in range(1, SIZE_X):
-        remote(mine, mine, send_x.at[d - 1], recv_x.at[d - 1], at_x(d)).start()
-    remote(mine, mine, send_c.at[0], recv_c.at[0], sibling).start()
-    for d in range(1, SIZE_X):
-        other = ((x + SIZE_X - d) % SIZE_X) * 2 + core
-        remote(result.at[other], result.at[other], send_x.at[d - 1], recv_x.at[d - 1], at_x(d)).wait_recv()
-        remote(result.at[other], result.at[other], send_c.at[d], recv_c.at[d], sibling).start()
-    for d in range(SIZE_X):
-        other = ((x + SIZE_X - d) % SIZE_X) * 2 + 1 - core
-        remote(result.at[other], result.at[other], send_c.at[d], recv_c.at[d], sibling).wait_recv()
+        first_y(d, before_y(d)).wait_recv()
+    for d in (2, 1, 3):
+        then_x(d, x).start()
+    share_x(0, core).start()
+    for d in (1, 3, 2):
+        then_y(d, before_y(d)).wait_recv()
+        share_y(d, core).start()
+        then_x(d, before_x(d)).wait_recv()
+        share_x(d, core).start()
+    for d in (0, 1, 3, 2):
+        share_y(d, 1 - core).wait_recv()
+        share_x(d, 1 - core).wait_recv()
 
     for i in range(BLOCKS):
         for j in range(i, BLOCKS):
             owner, place = block_place(i, j)
-            whole[i * BLOCK : (i + 1) * BLOCK, j * BLOCK : (j + 1) * BLOCK] = result[owner, place * BLOCK : (place + 1) * BLOCK, :]
+            for row in range(0, BLOCK, PART_Z):
+                quarter, number = divmod((place * BLOCK + row) // PART_Z, OWNERS)
+                whole[i * BLOCK + row : i * BLOCK + row + PART_Z, j * BLOCK : (j + 1) * BLOCK] = result[
+                    owner // 2, owner % 2, quarter, number // GROUP, number // 2 % 2, number % 2
+                ]
 
     cholesky(whole, work)
     out_ref[...] = whole[:, pl.ds(pl.multiple_of(b * BLOCK, BLOCK), BLOCK)]
 
     for d in range(1, SIZE_Y):
         remote(from_y.at[0], from_y.at[0], send_y.at[d - 1], recv_y.at[d - 1], at_y(d)).wait_send()
-        remote(mine.at[pl.ds(0, PART_Y)], mine.at[pl.ds(0, PART_Y)], send_gy.at[d - 1], recv_gy.at[d - 1], at_y(d)).wait_send()
+        first_y(d, y).wait_send()
+        then_y(d, y).wait_send()
+    for d in range(1, SIZE_X):
+        first_x(d, x).wait_send()
+        then_x(d, x).wait_send()
+    for d in range(SIZE_X):
+        share_y(d, core).wait_send()
+        share_x(d, core).wait_send()
     for d in range(1, SIZE_Z):
         there = (z + d) % SIZE_Z
 
@@ -372,9 +444,17 @@
         def _():
             remote(from_z.at[0], from_z.at[0], send_z.at[d - 1], recv_z.at[d - 1], at_z(d)).wait_send()
 
-        @pl.when(z < OWNERS)
-        def _():
-            remote(from_z.at[0], from_z.at[0], send_gz.at[d - 1], recv_gz.at[d - 1], at_z(d)).wait_send()
+    @pl.when(z < OWNERS)
+    def _():
+        for d in range(1, SIZE_Z // GROUP):
+            far(z, d).wait_send()
+
+    for full in (True, False):
+
+        @pl.when((z % GROUP < 2) == full)
+        def _():
+            for d in range(1, GROUP):
+                near(z % GROUP, d, full).wait_send()
 
     for k in range(count):
         for copy in (*first_halo(k), *second_halo(k), to_left(k), to_right(k), on_left(k), on_right(k)):
@@ -382,10 +462,6 @@
         for slot in range(2):
             across(filtered, slot, k).wait_send()
         store(k).wait()
-    for d in range(1, SIZE_X):
-        remote(mine, mine, send_x.at[d - 1], recv_x.at[d - 1], at_x(d)).wait_send()
-    for d in range(SIZE_X):
-        remote(mine, mine, send_c.at[d], recv_c.at[d], sibling).wait_send()
 
 
 def cholesky(S, work):
@@ -444,7 +520,7 @@
             pltpu.VMEM((SIZE_Y - 1, PART_Y, BLOCK), jnp.float32),
             pltpu.VMEM((SIZE_Z - 1, PART_Z, BLOCK), jnp.float32),
             pltpu.VMEM((PART_Y, BLOCK), jnp.float32),
-            pltpu.VMEM((BLOCKS, ROWS, BLOCK), jnp.float32),
+            pltpu.VMEM((SIZE_X, 2, SIZE_Y, 3, 2, 2, PART_Z, BLOCK), jnp.float32),
             pltpu.VMEM((TOTAL, TOTAL), jnp.float32),
             pltpu.VMEM((BLOCK, 2 * BLOCK), jnp.float32),
             dma((1 + count,)),
@@ -454,13 +530,13 @@
             dma((2, count)), dma((2, count)),
             dma((SIZE_Y - 1,)), dma((SIZE_Y - 1,)),
             dma((SIZE_Z - 1,)), dma((SIZE_Z - 1,)),
-            dma((SIZE_Z - 1,)), dma((SIZE_Z - 1,)),
-            dma((SIZE_Y - 1,)), dma((SIZE_Y - 1,)),
-            dma((SIZE_X - 1,)), dma((SIZE_X - 1,)),
-            dma((SIZE_X,)), dma((SIZE_X,)),
+            dma((2, GROUP - 1)), dma((2, GROUP - 1)),
+            dma((2, SIZE_Y - 1)), dma((2, SIZE_Y - 1)),
+            dma((2, SIZE_X - 1)), dma((2, SIZE_X - 1)),
+            dma((2, SIZE_X)), dma((2, SIZE_X)),
         ],
         compiler_params=pltpu.CompilerParams(
-            collective_id=1, has_side_effects=True, vmem_limit_bytes=48 * 1024 * 1024
+            collective_id=1, has_side_effects=True, vmem_limit_bytes=60 * 1024 * 1024
         ),
         name="filtered_factor",
     )(orbitals, potential)
@@ -468,7 +544,7 @@
 
 def local(orbitals, potential):
     cells = orbitals.shape[0] * GY * GX * SIZE_Y * SIZE_Z
-    return filtered_factor(orbitals, potential.reshape(-1, GX).T, cells)
+    return filtered_factor(orbitals, potential, cells)
 
 
 def solution(mesh):

time: 185 us -> 171 us (0.924)
  Pallas kernels: 180 us -> 167 us
    pallas_call x1, Pallas kernels: 180 us -> 167 us  [filtered_factor(): pl.pallas_call(functools.partial(factor_kernel, 1.0 / cells), out_shape=(...]
where the time goes in v3:
time: 171 us; the launch traced here: 170 us
  Pallas kernels  167 us (98%)
  local copies, waits for them, and re-layouts  3.12 us (2%)
    pallas_call x1, Pallas kernels, filtered_factor(): pl.pallas_call(functools.partial(factor_kernel, 1.0 / cells), out_shape=(...  167 us

profile of v3, /device:TPU:1, one launch (start us, length us, event | category | flops | bytes accessed | tf_op | source)
XLA Modules:
  0.0 170.4 jit_solution(14915150422902496520)
XLA Ops:
  0.6 166.7 %filtered_factor.1 = (f32[2,32,32,128]{3,2,1,0:T(8,128)}, f32[1024,128]{1,0:T(8,128)}) custom-call(f32[2,32,32,128]{3,2,1,0:T(8,128)} %orbitals_ref.1, f32[2,1024]{1,0:T(2,128)} %potential_ref.1), custom_call_target="tpu_custom_call" | custom-call | tf_op jit(solution)/shard_map/filtered_factor/pallas_call | solution.py:507
  167.3 0.0 copy-start
  167.3 2.3 %copy.6 = f32[2,32,32,128]{3,2,1,0:T(8,128)} copy(f32[2,32,32,128]{3,2,1,0:T(8,128)} %get-tuple-element.4) | data formatting | bytes 2097152
  169.6 0.0 copy-done
  169.6 0.8 copy.7
Async XLA Ops:
  167.3 2.3 %copy-start = (f32[1024,128]{1,0:T(8,128)S(1)}, f32[1024,128]{1,0:T(8,128)}, u32[]{:S(2)}) copy-start(f32[1024,128]{1,0:T(8,128)} %get-tuple-element.5) | copy-start | bytes 1572868

commit v4 on v3

--- a/solution.py
+++ b/solution.py
@@ -28,8 +28,9 @@
 GROUP = 4
 TOTAL = BLOCK * BLOCKS
 
-CHUNKS = tuple((4 * i, 4) for i in range(7)) + ((28, 2), (30, 2))
-AHEAD = 2
+CHUNKS = tuple((2 * i, 2) for i in range(16))
+AHEAD = 4
+LAGS = (0, 2, 4, 6)
 
 MESH = pl.DeviceIdType.MESH
 HIGHEST = lax.Precision.HIGHEST
@@ -121,8 +122,8 @@
 
 
 def factor_kernel(
-    scale, orbitals_ref, potential_ref, filtered_ref, out_ref,
-    weight, slab, before, after, current, before_2, after_2, filtered, gathered, relay, part,
+    scale, orbitals_ref, potential_ref, filtered, out_ref,
+    weight, slab, before, after, current, before_2, after_2, gathered, relay, part,
     from_y, from_z, summed, result, whole, work,
     local_sem, send_h, recv_h, send_k, recv_k, send_o, recv_o, send_s, recv_s,
     send_y, recv_y, send_z, recv_z, send_gz, recv_gz, send_gy, recv_gy, send_x, recv_x, send_c, recv_c,
@@ -189,9 +190,6 @@
     def across(source, slot, k):
         return remote(source.at[:, rows(k)], gathered.at[2 * slot, :, rows(k)], send_s.at[slot, k], recv_s.at[slot, k], sibling)
 
-    def store(k):
-        return pltpu.make_async_copy(filtered.at[:, rows(k)], filtered_ref.at[:, rows(k)], local_sem.at[1 + k])
-
     for k in range(AHEAD):
         for copy in first_halo(k):
             copy.start()
@@ -240,7 +238,6 @@
         def _():
             across(filtered, 0, k).start()
 
-        store(k).start()
 
     def pass_on(k):
         to_left(k).wait_recv()
@@ -282,7 +279,7 @@
 
     def advance(k):
         order.append(k)
-        for lag, stage in enumerate(stages):
+        for lag, stage in zip(LAGS, stages):
             place = len(order) - 1 - lag
             if 0 <= place < count and order[place] is not None:
                 stage(order[place])
@@ -294,7 +291,7 @@
     advance(0)
     for k in range(count - AHEAD, count):
         advance(k)
-    for lag in range(1, len(stages)):
+    for _ in range(LAGS[-1]):
         advance(None)
 
     for j in range(1, KEPT):
@@ -461,7 +458,6 @@
             copy.wait_send()
         for slot in range(2):
             across(filtered, slot, k).wait_send()
-        store(k).wait()
 
 
 def cholesky(S, work):
@@ -510,10 +506,10 @@
             jax.ShapeDtypeStruct((2, GY, GX, BLOCK), jnp.float32),
             jax.ShapeDtypeStruct((TOTAL, BLOCK), jnp.float32),
         ),
-        in_specs=[pl.BlockSpec(memory_space=pl.ANY), pl.BlockSpec(memory_space=pltpu.VMEM)],
-        out_specs=(pl.BlockSpec(memory_space=pl.ANY), pl.BlockSpec(memory_space=pltpu.VMEM)),
+        in_specs=[pl.BlockSpec(memory_space=pltpu.HBM), pl.BlockSpec(memory_space=pltpu.VMEM)],
+        out_specs=(pl.BlockSpec(memory_space=pltpu.VMEM), pl.BlockSpec(memory_space=pltpu.VMEM)),
         scratch_shapes=[
-            field, field, field, field, field, field, field, field,
+            field, field, field, field, field, field, field,
             pltpu.VMEM((KEPT - 1, 2, GY, GX, BLOCK), jnp.float32),
             pltpu.VMEM((GY, GX, BLOCK), jnp.float32),
             pltpu.VMEM((ROWS, BLOCK), jnp.float32),
@@ -523,7 +519,7 @@
             pltpu.VMEM((SIZE_X, 2, SIZE_Y, 3, 2, 2, PART_Z, BLOCK), jnp.float32),
             pltpu.VMEM((TOTAL, TOTAL), jnp.float32),
             pltpu.VMEM((BLOCK, 2 * BLOCK), jnp.float32),
-            dma((1 + count,)),
+            dma((1,)),
             dma((2, count)), dma((2, count)),
             dma((2, count)), dma((2, count)),
             dma((4, count)), dma((4, count)),
@@ -536,7 +532,7 @@
             dma((2, SIZE_X)), dma((2, SIZE_X)),
         ],
         compiler_params=pltpu.CompilerParams(
-            collective_id=1, has_side_effects=True, vmem_limit_bytes=60 * 1024 * 1024
+            collective_id=1, has_side_effects=True, vmem_limit_bytes=40 * 1024 * 1024
         ),
         name="filtered_factor",
     )(orbitals, potential)

time: 171 us -> 167 us (0.977)
  Pallas kernels: 167 us -> 161 us
    pallas_call x1, Pallas kernels: 167 us -> 161 us  [filtered_factor(): pl.pallas_call(functools.partial(factor_kernel, 1.0 / cells), out_shape=(...]
    unnamed x4 -> x6, local copies, waits for them, and re-layouts: 3.12 us -> 3.68 us
where the time goes in v4:
time: 167 us; the launch traced here: 166 us
  Pallas kernels  161 us (96%)
  local copies, waits for them, and re-layouts  3.68 us (2%)
    pallas_call x1, Pallas kernels, filtered_factor(): pl.pallas_call(functools.partial(factor_kernel, 1.0 / cells), out_shape=(...  161 us
    unnamed x6, local copies, waits for them, and re-layouts  3.68 us

profile of v4, /device:TPU:1, one launch (start us, length us, event | category | flops | bytes accessed | tf_op | source)
XLA Modules:
  0.0 165.7 jit_solution(1743222005150819613)
XLA Ops:
  0.6 0.0 copy-start
  0.6 1.2 copy-done
  1.9 0.0 copy-start.1
  1.9 0.7 copy-done.1
  2.6 161.4 %filtered_factor.1 = (f32[2,32,32,128]{3,2,1,0:T(8,128)S(1)}, f32[1024,128]{1,0:T(8,128)S(1)}) custom-call(f32[2,32,32,128]{3,2,1,0:T(8,128)S(1)} %copy-done, f32[2,1024]{1,0:T(2,128)S(1)} %copy-done.1), custom_call_target="tpu_custom_call" | custom-call | tf_op jit(solution)/shard_map/filtered_factor/pallas_call | solution.py:503
  163.9 1.0 copy.6
  164.9 0.8 copy.7
Async XLA Ops:
  0.6 1.2 copy-start
  1.9 0.7 copy-start.1

commit v5 on v4

--- a/solution.py
+++ b/solution.py
@@ -124,9 +124,9 @@
 def factor_kernel(
     scale, orbitals_ref, potential_ref, filtered, out_ref,
     weight, slab, before, after, current, before_2, after_2, gathered, relay, part,
-    from_y, from_z, summed, result, whole, work,
+    from_y, from_z, summed, result, whole, work, first,
     local_sem, send_h, recv_h, send_k, recv_k, send_o, recv_o, send_s, recv_s,
-    send_y, recv_y, send_z, recv_z, send_gz, recv_gz, send_gy, recv_gy, send_x, recv_x, send_c, recv_c,
+    send_y, recv_y, send_z, recv_z, send_gz, recv_gz, send_gy, recv_gy, send_x, recv_x, send_c, recv_c, send_e, recv_e,
 ):
     g, b = lax.axis_index("grid"), lax.axis_index("orb")
     y, z = g // SIZE_Z, g % SIZE_Z
@@ -390,6 +390,15 @@
     def before_y(d):
         return (y + SIZE_Y - d) % SIZE_Y
 
+    def lead(phase, d, device):
+        return remote(first, first, send_e.at[phase, d - 1], recv_e.at[phase, d - 1], device)
+
+    @pl.when((b == 0) & (y == 0))
+    def _():
+        first[...] = result[0, 0, 0, 0:2]
+        for d in (2, 1, 3):
+            lead(0, d, at_y(d)).start()
+
     for d in (2, 1, 3):
         first_x(d, x).start()
         first_y(d, y).start()
@@ -403,25 +412,51 @@
     for d in (2, 1, 3):
         then_x(d, x).start()
     share_x(0, core).start()
-    for d in (1, 3, 2):
-        then_y(d, before_y(d)).wait_recv()
-        share_y(d, core).start()
-        then_x(d, before_x(d)).wait_recv()
-        share_x(d, core).start()
-    for d in (0, 1, 3, 2):
-        share_y(d, 1 - core).wait_recv()
-        share_x(d, 1 - core).wait_recv()
-
-    for i in range(BLOCKS):
-        for j in range(i, BLOCKS):
-            owner, place = block_place(i, j)
-            for row in range(0, BLOCK, PART_Z):
-                quarter, number = divmod((place * BLOCK + row) // PART_Z, OWNERS)
-                whole[i * BLOCK + row : i * BLOCK + row + PART_Z, j * BLOCK : (j + 1) * BLOCK] = result[
-                    owner // 2, owner % 2, quarter, number // GROUP, number // 2 % 2, number % 2
-                ]
-
-    cholesky(whole, work)
+    for d in range(1, SIZE_Y):
+
+        @pl.when((b == 0) & (y == d))
+        def _():
+            lead(0, d, at_y(d)).wait_recv()
+
+    @pl.when(b == 0)
+    def _():
+        for d in (2, 1, 3):
+            lead(1, d, at_x(d)).start()
+
+    for d in range(1, SIZE_X):
+
+        @pl.when((core == 0) & (x == d))
+        def _():
+            lead(1, d, at_x(d)).wait_recv()
+
+    @pl.when(core == 0)
+    def _():
+        lead(2, 1, sibling).start()
+
+    @pl.when(core == 1)
+    def _():
+        lead(2, 1, sibling).wait_recv()
+
+    def finish():
+        for d in (1, 3, 2):
+            then_y(d, before_y(d)).wait_recv()
+            share_y(d, core).start()
+            then_x(d, before_x(d)).wait_recv()
+            share_x(d, core).start()
+        for d in (0, 1, 3, 2):
+            share_y(d, 1 - core).wait_recv()
+            share_x(d, 1 - core).wait_recv()
+
+        for i in range(BLOCKS):
+            for j in range(i, BLOCKS):
+                owner, place = block_place(i, j)
+                for row in range(0, BLOCK, PART_Z):
+                    quarter, number = divmod((place * BLOCK + row) // PART_Z, OWNERS)
+                    whole[i * BLOCK + row : i * BLOCK + row + PART_Z, j * BLOCK : (j + 1) * BLOCK] = result[
+                        owner // 2, owner % 2, quarter, number // GROUP, number // 2 % 2, number % 2
+                    ]
+
+    cholesky(whole, work, first, finish)
     out_ref[...] = whole[:, pl.ds(pl.multiple_of(b * BLOCK, BLOCK), BLOCK)]
 
     for d in range(1, SIZE_Y):
@@ -453,6 +488,20 @@
             for d in range(1, GROUP):
                 near(z % GROUP, d, full).wait_send()
 
+    @pl.when((b == 0) & (y == 0))
+    def _():
+        for d in range(1, SIZE_Y):
+            lead(0, d, at_y(d)).wait_send()
+
+    @pl.when(b == 0)
+    def _():
+        for d in range(1, SIZE_X):
+            lead(1, d, at_x(d)).wait_send()
+
+    @pl.when(core == 0)
+    def _():
+        lead(2, 1, sibling).wait_send()
+
     for k in range(count):
         for copy in (*first_halo(k), *second_halo(k), to_left(k), to_right(k), on_left(k), on_right(k)):
             copy.wait_send()
@@ -460,7 +509,7 @@
             across(filtered, slot, k).wait_send()
 
 
-def cholesky(S, work):
+def cholesky(S, work, first, finish):
     row = lax.broadcasted_iota(jnp.int32, (BLOCK, BLOCK), 0)
     column = lax.broadcasted_iota(jnp.int32, (BLOCK, BLOCK), 1)
 
@@ -469,10 +518,18 @@
 
             @pl.when(k == kk)
             def _():
-                work[:, 0:BLOCK] = S[kk * BLOCK : (kk + 1) * BLOCK, kk * BLOCK : (kk + 1) * BLOCK]
+                if kk == 0:
+                    work[:, 0:BLOCK] = first[...].reshape(BLOCK, BLOCK)
+                else:
+                    work[:, 0:BLOCK] = S[kk * BLOCK : (kk + 1) * BLOCK, kk * BLOCK : (kk + 1) * BLOCK]
 
         work[:, BLOCK:] = jnp.where(row == column, 1.0, 0.0)
         factor_diagonal(work)
+
+        @pl.when(k == 0)
+        def _():
+            finish()
+
         for kk in range(BLOCKS):
 
             @pl.when(k == kk)
@@ -519,6 +576,7 @@
             pltpu.VMEM((SIZE_X, 2, SIZE_Y, 3, 2, 2, PART_Z, BLOCK), jnp.float32),
             pltpu.VMEM((TOTAL, TOTAL), jnp.float32),
             pltpu.VMEM((BLOCK, 2 * BLOCK), jnp.float32),
+            pltpu.VMEM((2, 2, 2, PART_Z, BLOCK), jnp.float32),
             dma((1,)),
             dma((2, count)), dma((2, count)),
             dma((2, count)), dma((2, count)),
@@ -530,6 +588,7 @@
             dma((2, SIZE_Y - 1)), dma((2, SIZE_Y - 1)),
             dma((2, SIZE_X - 1)), dma((2, SIZE_X - 1)),
             dma((2, SIZE_X)), dma((2, SIZE_X)),
+            dma((3, 3)), dma((3, 3)),
         ],
         compiler_params=pltpu.CompilerParams(
             collective_id=1, has_side_effects=True, vmem_limit_bytes=40 * 1024 * 1024

time: 167 us -> 167 us (level)
  the two profiles are of different devices: /device:TPU:1 before, /device:TPU:2 now
where the time goes in v5:
time: 167 us
  Pallas kernels  163 us (98%)
  local copies, waits for them, and re-layouts  3.68 us (2%)
    pallas_call x1, Pallas kernels, filtered_factor(): pl.pallas_call(functools.partial(factor_kernel, 1.0 / cells), out_shape=(...  163 us
    unnamed x6, local copies, waits for them, and re-layouts  3.68 us

profile of v5, /device:TPU:2, one launch (start us, length us, event | category | flops | bytes accessed | tf_op | source)
XLA Modules:
  0.0 167.2 jit_solution(12167812994961292886)
XLA Ops:
  0.6 0.0 copy-start
  0.6 1.2 copy-done
  1.9 0.0 copy-start.1
  1.9 0.7 copy-done.1
  2.6 162.9 %filtered_factor.1 = (f32[2,32,32,128]{3,2,1,0:T(8,128)S(1)}, f32[1024,128]{1,0:T(8,128)S(1)}) custom-call(f32[2,32,32,128]{3,2,1,0:T(8,128)S(1)} %copy-done, f32[2,1024]{1,0:T(2,128)S(1)} %copy-done.1), custom_call_target="tpu_custom_call" | custom-call | tf_op jit(solution)/shard_map/filtered_factor/pallas_call | solution.py:560
  165.5 1.0 copy.6
  166.5 0.8 copy.7
Async XLA Ops:
  0.6 1.2 copy-start
  1.9 0.7 copy-start.1
